TPU v7x, 32 devices: a whole 2x2x4 slice. The times are simulated.
32 devices in a mesh: pipe: 4 (over z), ctx: 4 (over y, core), tp: 2 (over x).
Axes of the slice: x: 2, y: 2, z: 4, core: 2. Of those that a mesh axis runs over, the one named last changes fastest.
Arguments:
- queries: bfloat16 [4, 1024, 8192], P('pipe', 'ctx', 'tp'), may hold values from -16 to 16
- key_codes: bfloat16 [4, 1024, 512], P('pipe', 'ctx', 'tp'), may hold values from -127 to 127
- value_codes: bfloat16 [4, 1024, 512], P('pipe', 'ctx', 'tp'), may hold values from -127 to 127
- kv_scales: float32 [4, 8, 8], P('pipe', 'ctx'), may hold values from 0.004 to 0.032
- saved_out: bfloat16 [4, 1024, 8192], P('pipe', 'ctx', 'tp'), may hold values from -6 to 6
- section_grads: bfloat16 [4, 1024, 8192], P('pipe', 'ctx', 'tp'), may hold values from -6 to 6
- block_order: int32 [8], replicated, may hold values from 0 to 7, as said below
- block_docs: int32 [8], replicated, may hold values from 0 to 2, never falling along the last dimension, each value on 1 to 5 neighbouring positions
Outputs:
- grad_queries: bfloat16 [4, 1024, 8192], P('pipe', 'ctx', 'tp')
- grad_keys: bfloat16 [4, 1024, 512], P('pipe', ('ctx', 'tp'))
- grad_values: bfloat16 [4, 1024, 512], P('pipe', ('ctx', 'tp'))
Inputs may be any that keep to these rules, and one draw needn't show every extreme that they name: `block_order`: a permutation of the 8 sequence blocks; stored blocks 2 d and 2 d + 1 are sequence blocks p and 7 - p for some p.
All inputs are finite; a program needn't handle non-finite values.
Results may differ from a plain program's by a relative error of at most 0.0072.
Values may be sent and summed in bfloat16 or wider, within the bound.
A program may use at most 192 MiB of HBM per device.

v0:
```python
import jax
import jax.numpy as jnp
from jax import lax
from jax.sharding import PartitionSpec as P

HQ = 64
KVH = 4
HD = 128


masked_floor = -1e30


def from_behind(array, axis, by):
    size = lax.axis_size(axis)
    return lax.ppermute(array, axis, [(i, (i + by) % size) for i in range(size)])


def dequantize(codes, scales, block_rows, kv_here):
    rows_here = codes.shape[0]
    expanded = jnp.repeat(scales, block_rows, axis=0)
    values = codes.astype(jnp.float32).reshape(rows_here, kv_here, HD) * expanded[:, :, None]
    return values.astype(jnp.bfloat16).reshape(rows_here, kv_here * HD)


def on_device(
    queries, key_codes, value_codes, kv_scales, saved_out, section_grads, block_order, block_docs
):
    rows_here = queries.shape[1]
    block_rows = rows_here // 2
    kv_here = key_codes.shape[2] // HD
    repeats = HQ // KVH
    heads_here = queries.shape[2] // HD
    width_kv = kv_here * HD
    cycle_size = lax.axis_size("ctx")
    cycle_index = lax.axis_index("ctx")
    head_index = lax.axis_index("tp")
    inverse = HD ** (-0.5)
    incoming = from_behind(section_grads, "pipe", -1)
    key_scale = lax.dynamic_slice_in_dim(kv_scales[0], head_index * kv_here, kv_here, 1)
    value_scale = lax.dynamic_slice_in_dim(kv_scales[0], KVH + head_index * kv_here, kv_here, 1)
    keys = dequantize(key_codes[0], key_scale, block_rows, kv_here)
    values = dequantize(value_codes[0], value_scale, block_rows, kv_here)
    key_value = jnp.stack([keys, values])
    query = queries[0].reshape(rows_here, kv_here, repeats, HD)
    grad_out = incoming[0].reshape(rows_here, kv_here, repeats, HD)
    forward_out = saved_out[0].reshape(rows_here, kv_here, repeats, HD)
    block_ids = jnp.arange(block_order.shape[0], dtype=jnp.int32)

    def seq_block(rows):
        hit = (rows // block_rows)[:, None] == block_ids[None, :]
        return jnp.sum(jnp.where(hit, block_order[None, :], 0), axis=1)

    def document(blocks):
        hit = blocks[:, None] == block_ids[None, :]
        return jnp.sum(jnp.where(hit, block_docs[None, :], 0), axis=1)

    query_rows = cycle_index * rows_here + jnp.arange(rows_here, dtype=jnp.int32)
    query_block = seq_block(query_rows)
    query_pos = query_block * block_rows + query_rows % block_rows
    query_doc = document(query_block)

    def allowed(offset, count_rows):
        key_rows = offset + jnp.arange(count_rows, dtype=jnp.int32)
        key_block = seq_block(key_rows)
        key_pos = key_block * block_rows + key_rows % block_rows
        key_doc = document(key_block)
        return (key_pos[None, :] <= query_pos[:, None]) & (key_doc[None, :] == query_doc[:, None])

    def logits(key_piece):
        shaped = key_piece.reshape(-1, kv_here, HD)
        return (
            jnp.einsum("igrd,jgd->grij", query, shaped, preferred_element_type=jnp.float32)
            * inverse
        )

    piece = lax.all_gather(keys, "ctx", axis=0, tiled=True)
    running_max = jnp.full((kv_here, repeats, rows_here), masked_floor, jnp.float32)
    scores = logits(piece)
    visible = allowed(jnp.int32(0), piece.shape[0])[None, None]
    new_max = jnp.maximum(running_max, jnp.max(jnp.where(visible, scores, masked_floor), axis=-1))
    weights = jnp.where(visible, jnp.exp(scores - new_max[..., None]), 0.0)
    new_sum = jnp.sum(weights, axis=-1)
    log_norm = new_max + jnp.log(new_sum)
    row_dots = jnp.transpose(
        jnp.sum(grad_out.astype(jnp.float32) * forward_out.astype(jnp.float32), axis=-1), (1, 2, 0)
    )

    def block_grads(pair_block, offset):
        key_piece = pair_block[0].reshape(rows_here, kv_here, HD)
        value_piece = pair_block[1].reshape(rows_here, kv_here, HD)
        scores = logits(pair_block[0])
        visible = allowed(offset, rows_here)[None, None]
        probs = jnp.where(visible, jnp.exp(scores - log_norm[..., None]), 0.0)
        dprobs = jnp.einsum(
            "igrd,jgd->grij", grad_out, value_piece, preferred_element_type=jnp.float32
        )
        dscores = (probs * (dprobs - row_dots[..., None]) * inverse).astype(jnp.bfloat16)
        probs_low = probs.astype(jnp.bfloat16)
        grad_query = jnp.einsum(
            "grij,jgd->igrd", dscores, key_piece, preferred_element_type=jnp.float32
        )
        grad_key = jnp.einsum("grij,igrd->jgd", dscores, query, preferred_element_type=jnp.float32)
        grad_value = jnp.einsum(
            "grij,igrd->jgd", probs_low, grad_out, preferred_element_type=jnp.float32
        )
        return (
            grad_query,
            jnp.stack(
                [grad_key.reshape(rows_here, width_kv), grad_value.reshape(rows_here, width_kv)]
            ),
        )

    def anchor_slot(turn_index):
        return (cycle_index - turn_index) % cycle_size

    def advance(turn_index, carried, final_turn):
        current, partial_grads, grad_query = carried
        slot = anchor_slot(turn_index)
        query_term, pair_term = block_grads(current, slot * rows_here)
        grad_query = grad_query + query_term
        partial_grads = from_behind(partial_grads + pair_term, "ctx", 1)
        if not final_turn:
            current = from_behind(current, "ctx", 1)
        return (current, partial_grads, grad_query)

    start_grads = jnp.zeros((2, rows_here, width_kv), jnp.float32)
    start_query = jnp.zeros((rows_here, kv_here, repeats, HD), jnp.float32)
    carried = (key_value, start_grads, start_query)
    carried = lax.fori_loop(
        0,
        cycle_size - 1,
        lambda turn_index, state_now: advance(turn_index, state_now, False),
        carried,
    )
    carried = advance(cycle_size - 1, carried, True)
    current, partial_grads, grad_query = carried
    rounded = partial_grads.astype(jnp.bfloat16)
    regrouped = lax.all_to_all(rounded, "tp", split_axis=1, concat_axis=2, tiled=True)
    grad_queries = grad_query.astype(jnp.bfloat16).reshape(1, rows_here, heads_here * HD)
    grad_keys = regrouped[0][None]
    grad_values = regrouped[1][None]
    return (grad_queries, grad_keys, grad_values)


def solution(mesh):
    in_specs = (
        P("pipe", "ctx", "tp"),
        P("pipe", "ctx", "tp"),
        P("pipe", "ctx", "tp"),
        P("pipe", "ctx", None),
        P("pipe", "ctx", "tp"),
        P("pipe", "ctx", "tp"),
        P(),
        P(),
    )
    out_specs = (
        P("pipe", "ctx", "tp"),
        P("pipe", ("ctx", "tp"), None),
        P("pipe", ("ctx", "tp"), None),
    )
    return jax.shard_map(
        on_device, mesh=mesh, in_specs=in_specs, out_specs=out_specs, check_vma=False
    )
```

profile of v0, /device:TPU:0, one launch (start us, length us, event | category | flops | bytes accessed | tf_op | source)
XLA Modules:
  0.0 167.9 jit_solution(13207759231250277371)
XLA Ops:
  0.7 4.1 %copy.101 = bf16[1,256,4096]{1,2,0:T(8,128)(2,1)} copy(bf16[1,256,4096]{2,1,0:T(8,128)(2,1)} %param.15) | data formatting | bytes 4194304 | tf_op args[5]
  4.8 5.0 %collective-permute-start.2 = (bf16[1,256,4096]{1,2,0:T(8,128)(2,1)}, bf16[1,256,4096]{1,2,0:T(8,128)(2,1)}, u32[]{:S(2)}, u32[]{:S(2)}) collective-permute-start(bf16[1,256,4096]{1,2,0:T(8,128)(2,1)} %copy.101), channel_id=1, source_target_pairs={{0,24},{8,0},{16,8},{24,16},{1,25},{9,1},{17,9},{25,17},{2,26},{10... | collective-permute-start | bytes 6291464 | tf_op jit(solution)/shard_map/ppermute | solution.py:16
  10.7 7.2 %all_gather.3 = bf16[1024,256]{0,1:T(8,128)(2,1)S(1)} all-gather(bf16[256,256]{0,1:T(8,128)(2,1)S(1)} %fusion.32), channel_id=1, replica_groups=mesh['pipe'=4,'ctx'=4,'tp'=2] {'ctx'}, dimensions={0}, use_global_device_ids=true | all-gather | bytes 655360 | tf_op jit(solution)/shard_map/all_gather | solution.py:77
  17.9 3.3 %copy.98 = bf16[1,256,4096]{1,2,0:T(8,128)(2,1)S(1)} copy(bf16[1,256,4096]{2,1,0:T(8,128)(2,1)} %param.10) | data formatting | bytes 4194304 | tf_op args[0]
  21.6 13.4 %fusion.15 = (f32[2,16,256]{2,1,0:T(8,128)S(1)}, f32[2,1024,256,16]{2,1,3,0:T(8,128)}) fusion(pred[256,1024]{0,1:T(8,128)(4,1)S(1)} %compare_and_fusion.1, bf16[1024,2,128,1]{0,2,3,1:T(8,128)(2,1)S(1)} %bitcast.213, bf16[256,2,16,128]{0,3,2,1:T(8,128)(2,1)S(1)} %bitcast.203), kind=kOutput, calls=%fused_computation.31 | convolution fusion | flops 2172641280 | bytes 36470784 | tf_op jit(solution)/shard_map/igrd,jgd->grij/dot_general | solution.py:73
  35.3 4.1 %copy.102 = bf16[1,256,4096]{1,2,0:T(8,128)(2,1)} copy(bf16[1,256,4096]{2,1,0:T(8,128)(2,1)} %param.14) | data formatting | bytes 4194304 | tf_op args[4]
  39.4 0.7 pad_maximum_fusion
  40.1 0.8 compare_and_fusion.2
  40.9 14.6 %fusion.18 = f32[2,16,256]{2,1,0:T(8,128)S(1)} fusion(f32[2,1024,256,16]{2,1,3,0:T(8,128)} %get-tuple-element.527, f32[2,16,256]{2,1,0:T(8,128)S(1)} %broadcast_maximum_fusion, pred[256,1024]{0,1:T(8,128)(4,1)S(1)} %compare_and_fusion.1), kind=kLoop, calls=%fused_computation.34 | loop fusion | flops 33546240 | bytes 33882112 | tf_op jit(solution)/shard_map/reduce_sum | solution.py:83
  56.1 3.0 %fusion.25 = f32[256,2,16]{0,2,1:T(8,128)} fusion(bf16[256,2,16,128]{0,3,2,1:T(8,128)(2,1)S(1)} %bitcast.209, bf16[256,2,16,128]{0,3,2,1:T(8,128)(2,1)} %bitcast.10), kind=kLoop, calls=%fused_computation.44 | loop fusion | flops 4186112 | bytes 4227072 | tf_op jit(solution)/shard_map/reduce_sum | solution.py:86
  59.1 69.1 %while.22 = (s32[]{:T(128)}, bf16[2,256,256]{1,2,0:T(8,128)(2,1)}, f32[2,256,256]{1,2,0:T(8,128)S(1)}, f32[256,2,16,128]{3,0,2,1:T(8,128)}, s32[]{:T(128)}, /*in...) while((s32[]{:T(128)}, bf16[2,256,256]{1,2,0:T(8,128)(2,1)}, ...), condition=%wide.region_10.11_spmd.clone.clone, body=%wide.region_7.10_spmd.clone.clone.sunk | while | flops 2709998592 | bytes 78294504 | solution.py:130
  59.3 1.0 copy.162
  60.9 1.3 fusion.103
  62.3 3.3 %fusion.105 = f32[2,256,128,1]{1,2,3,0:T(8,128)S(1)} fusion(bf16[256,2,16,128]{0,3,2,1:T(8,128)(2,1)} %get-tuple-element.660, f32[2,256,256,16]{2,1,3,0:T(8,128)S(1)} %fusion.103, f32[2,16,256]{2,1,0:T(8,128)} %get-tuple-element.659, pred[256,256]{0,1:T(8,128)(4,1)S(1)} %compare_and_fusion.4), kind=kOutput, calls=%fused_computation.10.clone.1 | convolution fusion | flops 545259520 | bytes 10846208 | tf_op jit(solution)/shard_map/while/body/eval_jaxpr/grij,igrd->jgd/dot_general | solution.py:104
  65.6 4.7 %fusion.106 = bf16[2,16,256,256]{2,3,1,0:T(8,128)(2,1)S(1)} fusion(f32[2,256,256,16]{2,1,3,0:T(8,128)S(1)} %fusion.103, f32[2,16,256]{2,1,0:T(8,128)} %get-tuple-element.661, f32[2,16,256]{2,1,0:T(8,128)} %get-tuple-element.659, pred[256,256]{0,1:T(8,128)(4,1)S(1)} %compare_and_fusion.4, bf16[256,2,128,1]{0,2,3,1:T(8,128)(2,1)S(1)} %bitcast.211, ...), kind=kOutput, calls=%fused_computation.4.clone.1 | convolution fusion | flops 551550976 | bytes 14942208 | tf_op jit(solution)/shard_map/while/body/eval_jaxpr/igrd,jgd->grij/dot_general | solution.py:95
  70.4 1.9 %copy-done = bf16[2,16,256,256]{2,3,1,0:T(8,128)(2,1)} copy-done((bf16[2,16,256,256]{2,3,1,0:T(8,128)(2,1)}, bf16[2,16,256,256]{2,3,1,0:T(8,128)(2,1)S(1)}, u32[]{:S(2)}) %copy-start) | copy-done | bytes 4194328 | tf_op jit(solution)/shard_map/while
  72.3 1.4 fusion.107
  73.8 0.6 collective-permute-start.1
  74.5 6.0 %bitcast_add_fusion.3 = f32[256,2,16,128]{3,0,2,1:T(8,128)} fusion(f32[256,2,16,128]{3,0,2,1:T(8,128)} %get-tuple-element.634, bf16[2,16,256,256]{2,3,1,0:T(8,128)(2,1)} %copy-done, bf16[256,2,128,1]{0,2,3,1:T(8,128)(2,1)S(1)} %bitcast.206, pred[]{:T(512)S(6)} %compare.52), kind=kOutput, calls=%fused_computation.9.clone.1 | convolution fusion | flops 538968064 | bytes 12713985 | tf_op jit(solution)/shard_map/while/body/eval_jaxpr/grij,jgd->igrd/dot_general | solution.py:100
  80.5 2.0 %collective-permute-done.1 = f32[2,256,256]{1,2,0:T(8,128)S(1)} collective-permute-done((f32[2,256,256]{1,2,0:T(8,128)S(1)}, f32[2,256,256]{1,2,0:T(8,128)S(1)}, u32[]{:S(2)}, u32[]{:S(2)}) %collective-permute-start.1) | collective-permute-done | bytes 524320 | tf_op jit(solution)/shard_map/while/body/eval_jaxpr/ppermute | solution.py:16
  82.5 1.0 copy.162
  83.7 1.3 fusion.103
  85.1 3.3 %fusion.105 = f32[2,256,128,1]{1,2,3,0:T(8,128)S(1)} fusion(bf16[256,2,16,128]{0,3,2,1:T(8,128)(2,1)} %get-tuple-element.660, f32[2,256,256,16]{2,1,3,0:T(8,128)S(1)} %fusion.103, f32[2,16,256]{2,1,0:T(8,128)} %get-tuple-element.659, pred[256,256]{0,1:T(8,128)(4,1)S(1)} %compare_and_fusion.4), kind=kOutput, calls=%fused_computation.10.clone.1 | convolution fusion | flops 545259520 | bytes 10846208 | tf_op jit(solution)/shard_map/while/body/eval_jaxpr/grij,igrd->jgd/dot_general | solution.py:104
  88.5 4.8 %fusion.106 = bf16[2,16,256,256]{2,3,1,0:T(8,128)(2,1)S(1)} fusion(f32[2,256,256,16]{2,1,3,0:T(8,128)S(1)} %fusion.103, f32[2,16,256]{2,1,0:T(8,128)} %get-tuple-element.661, f32[2,16,256]{2,1,0:T(8,128)} %get-tuple-element.659, pred[256,256]{0,1:T(8,128)(4,1)S(1)} %compare_and_fusion.4, bf16[256,2,128,1]{0,2,3,1:T(8,128)(2,1)S(1)} %bitcast.211, ...), kind=kOutput, calls=%fused_computation.4.clone.1 | convolution fusion | flops 551550976 | bytes 14942208 | tf_op jit(solution)/shard_map/while/body/eval_jaxpr/igrd,jgd->grij/dot_general | solution.py:95
  93.2 1.9 %copy-done = bf16[2,16,256,256]{2,3,1,0:T(8,128)(2,1)} copy-done((bf16[2,16,256,256]{2,3,1,0:T(8,128)(2,1)}, bf16[2,16,256,256]{2,3,1,0:T(8,128)(2,1)S(1)}, u32[]{:S(2)}) %copy-start) | copy-done | bytes 4194328 | tf_op jit(solution)/shard_map/while
  95.2 1.4 fusion.107
  96.7 1.0 collective-permute-start.1
  97.7 7.3 %bitcast_add_fusion.3 = f32[256,2,16,128]{3,0,2,1:T(8,128)} fusion(f32[256,2,16,128]{3,0,2,1:T(8,128)} %get-tuple-element.634, bf16[2,16,256,256]{2,3,1,0:T(8,128)(2,1)} %copy-done, bf16[256,2,128,1]{0,2,3,1:T(8,128)(2,1)S(1)} %bitcast.206, pred[]{:T(512)S(6)} %compare.52), kind=kOutput, calls=%fused_computation.9.clone.1 | convolution fusion | flops 538968064 | bytes 12713985 | tf_op jit(solution)/shard_map/while/body/eval_jaxpr/grij,jgd->igrd/dot_general | solution.py:100
  105.3 1.0 copy.162
  106.5 1.3 fusion.103
  108.0 3.3 %fusion.105 = f32[2,256,128,1]{1,2,3,0:T(8,128)S(1)} fusion(bf16[256,2,16,128]{0,3,2,1:T(8,128)(2,1)} %get-tuple-element.660, f32[2,256,256,16]{2,1,3,0:T(8,128)S(1)} %fusion.103, f32[2,16,256]{2,1,0:T(8,128)} %get-tuple-element.659, pred[256,256]{0,1:T(8,128)(4,1)S(1)} %compare_and_fusion.4), kind=kOutput, calls=%fused_computation.10.clone.1 | convolution fusion | flops 545259520 | bytes 10846208 | tf_op jit(solution)/shard_map/while/body/eval_jaxpr/grij,igrd->jgd/dot_general | solution.py:104
  111.3 4.7 %fusion.106 = bf16[2,16,256,256]{2,3,1,0:T(8,128)(2,1)S(1)} fusion(f32[2,256,256,16]{2,1,3,0:T(8,128)S(1)} %fusion.103, f32[2,16,256]{2,1,0:T(8,128)} %get-tuple-element.661, f32[2,16,256]{2,1,0:T(8,128)} %get-tuple-element.659, pred[256,256]{0,1:T(8,128)(4,1)S(1)} %compare_and_fusion.4, bf16[256,2,128,1]{0,2,3,1:T(8,128)(2,1)S(1)} %bitcast.211, ...), kind=kOutput, calls=%fused_computation.4.clone.1 | convolution fusion | flops 551550976 | bytes 14942208 | tf_op jit(solution)/shard_map/while/body/eval_jaxpr/igrd,jgd->grij/dot_general | solution.py:95
  116.1 1.9 %copy-done = bf16[2,16,256,256]{2,3,1,0:T(8,128)(2,1)} copy-done((bf16[2,16,256,256]{2,3,1,0:T(8,128)(2,1)}, bf16[2,16,256,256]{2,3,1,0:T(8,128)(2,1)S(1)}, u32[]{:S(2)}) %copy-start) | copy-done | bytes 4194328 | tf_op jit(solution)/shard_map/while
  118.0 1.4 fusion.107
  119.5 1.0 collective-permute-start.1
  120.5 7.3 %bitcast_add_fusion.3 = f32[256,2,16,128]{3,0,2,1:T(8,128)} fusion(f32[256,2,16,128]{3,0,2,1:T(8,128)} %get-tuple-element.634, bf16[2,16,256,256]{2,3,1,0:T(8,128)(2,1)} %copy-done, bf16[256,2,128,1]{0,2,3,1:T(8,128)(2,1)S(1)} %bitcast.206, pred[]{:T(512)S(6)} %compare.52), kind=kOutput, calls=%fused_computation.9.clone.1 | convolution fusion | flops 538968064 | bytes 12713985 | tf_op jit(solution)/shard_map/while/body/eval_jaxpr/grij,jgd->igrd/dot_general | solution.py:100
  128.2 1.0 fusion.50
  129.2 1.3 fusion.53
  130.5 4.9 %fusion.27 = f32[2,256,128,1]{1,2,3,0:T(8,128)S(1)} fusion(bf16[256,2,16,128]{0,3,2,1:T(8,128)(2,1)} %bitcast.10, f32[2,256,256,16]{2,1,3,0:T(8,128)S(1)} %fusion.53, f32[2,16,256]{2,1,0:T(8,128)} %log_add_fusion, pred[256,256]{0,1:T(8,128)(4,1)S(1)} %copy-done.6), kind=kOutput, calls=%fused_computation.47 | convolution fusion | flops 545259520 | bytes 10846208 | tf_op jit(solution)/shard_map/grij,igrd->jgd/dot_general | solution.py:104
  135.6 6.3 %fusion.21 = bf16[2,16,256,256]{2,3,1,0:T(8,128)(2,1)S(1)} fusion(f32[2,256,256,16]{2,1,3,0:T(8,128)} %copy-done.2, f32[2,16,256]{2,1,0:T(8,128)} %bitcast.12, f32[2,16,256]{2,1,0:T(8,128)} %log_add_fusion, pred[256,256]{0,1:T(8,128)(4,1)S(1)} %copy-done.6, bf16[256,2,128,1]{0,2,3,1:T(8,128)(2,1)S(1)} %bitcast.218, bf16[256,2,16,128]{0,3,2,1:T(8,128)(2,1)} %bitcast.10), kind=kOutput, calls=%fused_computation.38 | convolution fusion | flops 551550976 | bytes 14942208 | tf_op jit(solution)/shard_map/igrd,jgd->grij/dot_general | solution.py:95
  141.9 1.4 fusion.55
  144.9 5.4 %copy.108 = f32[256,2,16,128]{0,3,2,1:T(8,128)} copy(f32[256,2,16,128]{3,0,2,1:T(8,128)} %get-tuple-element.384) | data formatting | bytes 8388608 | tf_op jit(solution)/shard_map/while | solution.py:130
  150.3 4.9 %fusion.54 = f32[2,128,16,256]{3,1,2,0:T(8,128)} fusion(bf16[256,2,128,1]{0,2,3,1:T(8,128)(2,1)S(1)} %bitcast.215, bf16[2,16,256,256]{2,3,1,0:T(8,128)(2,1)} %copy-done.1), kind=kOutput, calls=%fused_computation.118 | convolution fusion | flops 536870912 | bytes 8519680 | tf_op jit(solution)/shard_map/grij,jgd->igrd/dot_general | solution.py:100
  155.2 3.4 %all-to-all-start = ((bf16[2,256,256]{2,0,1:T(2,128)(2,1)}), bf16[2,256,256]{2,0,1:T(2,128)(2,1)S(1)}, u32[]{:S(2)}, u32[]{:S(2)}) async-start(bf16[2,256,256]{2,0,1:T(2,128)(2,1)} %collective-permute-done.3), calls=%async_computation | async-start | bytes 524288 | tf_op jit(solution)/shard_map/all_to_all | solution.py:139
  158.6 4.1 %fusion.26 = bf16[256,2,16,128]{0,3,2,1:T(8,128)(2,1)S(1)} fusion(f32[256,2,16,128]{0,3,2,1:T(8,128)} %copy.108, f32[2,128,16,256]{3,1,2,0:T(8,128)} %fusion.54), kind=kLoop, calls=%fused_computation.46 | loop fusion | flops 2097152 | bytes 10485760 | tf_op jit(solution)/shard_map/convert_element_type | solution.py:140
  162.7 2.9 %copy.116 = bf16[1,256,4096]{2,1,0:T(8,128)(2,1)} copy(bf16[1,256,4096]{1,2,0:T(8,128)(2,1)S(1)} %bitcast.208) | data formatting | bytes 4194304
  166.2 0.7 slice.45
  167.1 0.7 slice.47
  (87 shorter events, 7.0 us)
Async XLA Ops:
  0.6 9.2 %copy-start.9 = (f32[1,2,8]{2,1,0:T(2,128)S(1)}, f32[1,2,8]{2,1,0:T(2,128)}, u32[]{:S(2)}) copy-start(f32[1,2,8]{2,1,0:T(2,128)} %param.13) | copy-start | bytes 196
  0.6 9.5 %copy-start.4 = (bf16[1,256,256]{2,1,0:T(8,128)(2,1)S(1)}, bf16[1,256,256]{2,1,0:T(8,128)(2,1)}, u32[]{:S(2)}) copy-start(bf16[1,256,256]{2,1,0:T(8,128)(2,1)} %param.11) | copy-start | bytes 393220
  0.7 9.7 %copy-start.7 = (s32[8]{0:T(128)S(1)}, s32[8]{0:T(128)}, u32[]{:S(2)}) copy-start(s32[8]{0:T(128)} %param.16) | copy-start | bytes 100
  0.7 9.9 %copy-start.8 = (s32[8]{0:T(128)S(1)}, s32[8]{0:T(128)}, u32[]{:S(2)}) copy-start(s32[8]{0:T(128)} %param.17) | copy-start | bytes 100
  4.8 51.3 %collective-permute-start.2 = (bf16[1,256,4096]{1,2,0:T(8,128)(2,1)}, bf16[1,256,4096]{1,2,0:T(8,128)(2,1)}, u32[]{:S(2)}, u32[]{:S(2)}) collective-permute-start(bf16[1,256,4096]{1,2,0:T(8,128)(2,1)} %copy.101), channel_id=1, source_target_pairs={{0,24},{8,0},{16,8},{24,16},{1,25},{9,1},{17,9},{25,17},{2,26},{10... | collective-permute-start | bytes 6291464 | tf_op jit(solution)/shard_map/ppermute | solution.py:16
  21.5 13.6 %copy-start.5 = (bf16[1,256,256]{2,1,0:T(8,128)(2,1)S(1)}, bf16[1,256,256]{2,1,0:T(8,128)(2,1)}, u32[]{:S(2)}) copy-start(bf16[1,256,256]{2,1,0:T(8,128)(2,1)} %param.12) | copy-start | bytes 393220
  40.9 15.2 %copy-start.3 = (bf16[1,256,4096]{1,2,0:T(8,128)(2,1)S(1)}, bf16[1,256,4096]{1,2,0:T(8,128)(2,1)}, u32[]{:S(2)}) copy-start(bf16[1,256,4096]{1,2,0:T(8,128)(2,1)} %copy.102) | copy-start | bytes 6291460
  60.3 20.2 %collective-permute-start = (bf16[2,256,256]{1,2,0:T(8,128)(2,1)S(1)}, bf16[2,256,256]{1,2,0:T(8,128)(2,1)}, u32[]{:S(2)}, u32[]{:S(2)}) collective-permute-start(bf16[2,256,256]{1,2,0:T(8,128)(2,1)S(1)} %copy.162), channel_id=1, source_target_pairs={{0,2},{2,4},{4,6},{6,0},{1,3},{3,5},{5,7},{7,1},{8,10},{10,12},{12... | collective-permute-start | bytes 786440 | tf_op jit(solution)/shard_map/while/body/eval_jaxpr/ppermute | solution.py:16
  70.4 1.9 %copy-start = (bf16[2,16,256,256]{2,3,1,0:T(8,128)(2,1)}, bf16[2,16,256,256]{2,3,1,0:T(8,128)(2,1)S(1)}, u32[]{:S(2)}) copy-start(bf16[2,16,256,256]{2,3,1,0:T(8,128)(2,1)S(1)} %fusion.106) | copy-start | bytes 12582916 | tf_op jit(solution)/shard_map/while
  73.8 8.7 %collective-permute-start.1 = (f32[2,256,256]{1,2,0:T(8,128)S(1)}, f32[2,256,256]{1,2,0:T(8,128)S(1)}, u32[]{:S(2)}, u32[]{:S(2)}) collective-permute-start(f32[2,256,256]{1,2,0:T(8,128)S(1)} %maximum_add_fusion.3), channel_id=1, source_target_pairs={{0,2},{2,4},{4,6},{6,0},{1,3},{3,5},{5,7},{7,1},{8,10},{10,12},{12... | collective-permute-start | bytes 1572872 | tf_op jit(solution)/shard_map/while/body/eval_jaxpr/ppermute | solution.py:16
  83.5 21.5 %collective-permute-start = (bf16[2,256,256]{1,2,0:T(8,128)(2,1)S(1)}, bf16[2,256,256]{1,2,0:T(8,128)(2,1)}, u32[]{:S(2)}, u32[]{:S(2)}) collective-permute-start(bf16[2,256,256]{1,2,0:T(8,128)(2,1)S(1)} %copy.162), channel_id=1, source_target_pairs={{0,2},{2,4},{4,6},{6,0},{1,3},{3,5},{5,7},{7,1},{8,10},{10,12},{12... | collective-permute-start | bytes 786440 | tf_op jit(solution)/shard_map/while/body/eval_jaxpr/ppermute | solution.py:16
  93.2 1.9 %copy-start = (bf16[2,16,256,256]{2,3,1,0:T(8,128)(2,1)}, bf16[2,16,256,256]{2,3,1,0:T(8,128)(2,1)S(1)}, u32[]{:S(2)}) copy-start(bf16[2,16,256,256]{2,3,1,0:T(8,128)(2,1)S(1)} %fusion.106) | copy-start | bytes 12582916 | tf_op jit(solution)/shard_map/while
  96.7 8.7 %collective-permute-start.1 = (f32[2,256,256]{1,2,0:T(8,128)S(1)}, f32[2,256,256]{1,2,0:T(8,128)S(1)}, u32[]{:S(2)}, u32[]{:S(2)}) collective-permute-start(f32[2,256,256]{1,2,0:T(8,128)S(1)} %maximum_add_fusion.3), channel_id=1, source_target_pairs={{0,2},{2,4},{4,6},{6,0},{1,3},{3,5},{5,7},{7,1},{8,10},{10,12},{12... | collective-permute-start | bytes 1572872 | tf_op jit(solution)/shard_map/while/body/eval_jaxpr/ppermute | solution.py:16
  106.3 21.5 %collective-permute-start = (bf16[2,256,256]{1,2,0:T(8,128)(2,1)S(1)}, bf16[2,256,256]{1,2,0:T(8,128)(2,1)}, u32[]{:S(2)}, u32[]{:S(2)}) collective-permute-start(bf16[2,256,256]{1,2,0:T(8,128)(2,1)S(1)} %copy.162), channel_id=1, source_target_pairs={{0,2},{2,4},{4,6},{6,0},{1,3},{3,5},{5,7},{7,1},{8,10},{10,12},{12... | collective-permute-start | bytes 786440 | tf_op jit(solution)/shard_map/while/body/eval_jaxpr/ppermute | solution.py:16
  116.1 1.9 %copy-start = (bf16[2,16,256,256]{2,3,1,0:T(8,128)(2,1)}, bf16[2,16,256,256]{2,3,1,0:T(8,128)(2,1)S(1)}, u32[]{:S(2)}) copy-start(bf16[2,16,256,256]{2,3,1,0:T(8,128)(2,1)S(1)} %fusion.106) | copy-start | bytes 12582916 | tf_op jit(solution)/shard_map/while
  119.5 8.7 %collective-permute-start.1 = (f32[2,256,256]{1,2,0:T(8,128)S(1)}, f32[2,256,256]{1,2,0:T(8,128)S(1)}, u32[]{:S(2)}, u32[]{:S(2)}) collective-permute-start(f32[2,256,256]{1,2,0:T(8,128)S(1)} %maximum_add_fusion.3), channel_id=1, source_target_pairs={{0,2},{2,4},{4,6},{6,0},{1,3},{3,5},{5,7},{7,1},{8,10},{10,12},{12... | collective-permute-start | bytes 1572872 | tf_op jit(solution)/shard_map/while/body/eval_jaxpr/ppermute | solution.py:16
  129.2 1.3 copy-start.6
  130.5 5.0 %copy-start.2 = (f32[2,256,256,16]{2,1,3,0:T(8,128)}, f32[2,256,256,16]{2,1,3,0:T(8,128)S(1)}, u32[]{:S(2)}) copy-start(f32[2,256,256,16]{2,1,3,0:T(8,128)S(1)} %fusion.53) | copy-start | bytes 25165828
  141.9 1.9 %copy-start.1 = (bf16[2,16,256,256]{2,3,1,0:T(8,128)(2,1)}, bf16[2,16,256,256]{2,3,1,0:T(8,128)(2,1)S(1)}, u32[]{:S(2)}) copy-start(bf16[2,16,256,256]{2,3,1,0:T(8,128)(2,1)S(1)} %fusion.21) | copy-start | bytes 12582916
  144.8 10.4 %collective-permute-start.3 = (bf16[2,256,256]{2,0,1:T(2,128)(2,1)S(1)}, bf16[2,256,256]{2,0,1:T(2,128)(2,1)}, u32[]{:S(2)}, u32[]{:S(2)}) collective-permute-start(bf16[2,256,256]{2,0,1:T(2,128)(2,1)S(1)} %maximum_add_fusion.1), channel_id=1, source_target_pairs={{0,2},{2,4},{4,6},{6,0},{1,3},{3,5},{5,7},{7,1},{8,10},{10,12},{12... | collective-permute-start | bytes 786440 | tf_op jit(solution)/shard_map/ppermute | solution.py:16
  155.2 10.4 %all-to-all-start = ((bf16[2,256,256]{2,0,1:T(2,128)(2,1)}), bf16[2,256,256]{2,0,1:T(2,128)(2,1)S(1)}, u32[]{:S(2)}, u32[]{:S(2)}) async-start(bf16[2,256,256]{2,0,1:T(2,128)(2,1)} %collective-permute-done.3), calls=%async_computation | async-start | bytes 524288 | tf_op jit(solution)/shard_map/all_to_all | solution.py:139
where the time goes:
time: 169 us; the launch traced here: 168 us
  matrix products  85.2 us (50%)
  local copies, waits for them, and re-layouts  33.4 us (20%)
  other arithmetic  26.4 us (16%)
  starting transfers between devices  11.5 us (7%)
  blocking collectives  7.2 us (4%)
  waiting for transfers between devices  2.86 us (2%)
    dot_general x4, matrix products, block_grads(): jnp.einsum('grij,jgd->igrd', dscores, key_piece, preferred_element_type=j...  25.4 us
    dot_general x4, matrix products, block_grads(): jnp.einsum('igrd,jgd->grij', grad_out, value_piece, preferred_element_typ...  20.5 us
    dot_general x5, matrix products, logits(): jnp.einsum('igrd,jgd->grij', query, shaped, preferred_element_type=jnp.fl...  18.6 us
    unnamed x28, local copies, waits for them, and re-layouts  15.2 us
    dot_general x4, matrix products, block_grads(): jnp.einsum('grij,igrd->jgd', probs_low, grad_out, preferred_element_type=...  15 us
    reduce_sum x1, other arithmetic, on_device(): new_sum = jnp.sum(weights, axis=-1)  14.6 us
    while x9, local copies, waits for them, and re-layouts  8.61 us
    ppermute x8, starting transfers between devices, from_behind(): lax.ppermute(array, axis, [(i, (i + by) % size) for i in range(size)])  8.09 us
  transfers between devices with their start and end apart: 9, of which 3 were waited for; matrix products, arithmetic and copies ran while one was open for 66% of the time, Pallas kernels for 0%

commit v1 on v0

v1 whole, which is shorter than its diff:
```python
import jax
import jax.numpy as jnp
from jax import lax
from jax.experimental import pallas as pl
from jax.experimental.pallas import tpu as pltpu
from jax.sharding import PartitionSpec as P

HQ = 64
KVH = 4
HD = 128
HEADS_AT_ONCE = 2

masked_floor = -1e30
MESH = pl.DeviceIdType.MESH
NT = (((1,), (1,)), ((), ()))
NN = (((1,), (0,)), ((), ()))


def dot(a, b, dims=NN):
    return lax.dot_general(a, b, dims, preferred_element_type=jnp.float32)


def make_kernel(sizes, rows, heads, kv_here, blocks):
    pipes, cycle, tps = sizes
    blk = rows // 2
    width = HEADS_AT_ONCE * HD
    chunks = heads // HEADS_AT_ONCE
    per_kv = chunks // kv_here
    supers = blocks // 2
    sure = blocks // 4 + 1
    floats = supers - sure
    tasks = sure + 1 + floats
    peers = cycle * tps
    inverse = HD ** (-0.5)

    def kernel(
        order_ref, docs_ref, scales_ref, key_codes, value_codes, queries, saved, grads,
        dq_out, dk_out, dv_out,
        q_buf, o_buf, do_buf, dq_buf, k_all, v_all, k_seq, v_seq, kt_seq, bias, probs,
        dk_acc, dv_acc, send_buf, recv_buf,
        q_sem, o_sem, dq_sem, z_send, z_recv, kv_send, kv_recv, g_send, g_recv,
    ):
        pipe = lax.axis_index("pipe")
        ctx = lax.axis_index("ctx")
        tp = lax.axis_index("tp")
        me = ctx * tps + tp
        ahead = lax.rem(pipe + 1, pipes)
        behind = lax.rem(pipe + pipes - 1, pipes)

        def peer(k):
            flat = lax.rem(me + k, peers)
            return flat, (pipe, flat // tps, lax.rem(flat, tps))

        barrier = pltpu.get_barrier_semaphore()
        for where in (ahead, behind):
            pl.semaphore_signal(barrier, inc=1, device_id=(where, ctx, tp), device_id_type=MESH)
        for k in range(1, peers):
            pl.semaphore_signal(barrier, inc=1, device_id=peer(k)[1], device_id_type=MESH)
        pl.semaphore_wait(barrier, peers + 1)

        def columns(ref, c):
            return ref.at[0, :, pl.ds(pl.multiple_of(c * width, width), width)]

        def z_copy(c):
            return pltpu.make_async_remote_copy(
                src_ref=columns(grads, c), dst_ref=do_buf.at[c],
                send_sem=z_send.at[c], recv_sem=z_recv.at[c],
                device_id=(behind, ctx, tp), device_id_type=MESH,
            )

        def q_copy(c):
            return pltpu.make_async_copy(columns(queries, c), q_buf.at[c], q_sem.at[c])

        def o_copy(c):
            return pltpu.make_async_copy(columns(saved, c), o_buf.at[c], o_sem.at[c])

        def dq_copy(c):
            return pltpu.make_async_copy(dq_buf.at[c], columns(dq_out, c), dq_sem.at[c])

        @pl.loop(0, chunks)
        def _(c):
            z_copy(c).start()

        @pl.loop(0, chunks)
        def _(c):
            q_copy(c).start()

        here = pl.ds(2 * ctx, 2)
        gathered = (k_all, v_all)
        for kind, codes in ((0, key_codes), (1, value_codes)):
            for half in range(2):
                for g in range(kv_here):
                    scale = scales_ref[0, half, kind * KVH + tp * kv_here + g]
                    piece = codes[0, half * blk:(half + 1) * blk, g * HD:(g + 1) * HD]
                    gathered[kind][2 * ctx + half, :, g * HD:(g + 1) * HD] = (
                        piece.astype(jnp.float32) * scale
                    ).astype(jnp.bfloat16)

        def kv_copy(kind, k):
            return pltpu.make_async_remote_copy(
                src_ref=gathered[kind].at[here], dst_ref=gathered[kind].at[here],
                send_sem=kv_send.at[kind, k], recv_sem=kv_recv.at[kind, k],
                device_id=(pipe, lax.rem(ctx + k, cycle), tp), device_id_type=MESH,
            )

        for kind in range(2):
            for k in range(1, cycle):
                kv_copy(kind, k).start()

        @pl.loop(0, chunks)
        def _(c):
            o_copy(c).start()

        first = order_ref[2 * ctx]
        second = order_ref[2 * ctx + 1]
        first_hi = jnp.minimum(jnp.maximum(first - second, 0), 1)
        hi_block = jnp.maximum(first, second)
        lo_block = jnp.minimum(first, second)
        lo_count = lax.div(lo_block + 2, 2)

        float_hi, float_super = [], []
        for f in range(floats):
            is_hi = jnp.minimum(jnp.maximum(f + 2 - lo_count, 0), 1)
            float_hi.append(is_hi)
            float_super.append(jnp.clip(1 + f + is_hi * (sure - lo_count), 0, supers - 1))

        def choose(flag, one, other):
            return jnp.where(jnp.full(one.shape, flag, jnp.int32) > 0, one, other)

        def super_of(t):
            if t < sure:
                return t
            return 0 if t == sure else float_super[t - sure - 1]

        def pick(t, hi, lo):
            if t < sure:
                return hi
            if t == sure:
                return lo
            flag = float_hi[t - sure - 1]
            if hi.shape == ():
                return flag * hi + (1 - flag) * lo
            return choose(flag, hi, lo)

        for t in range(tasks):
            m = super_of(t)
            block = pick(t, hi_block, lo_block)
            key = lax.broadcasted_iota(jnp.int32, (2 * blk, width), 0)
            row = lax.broadcasted_iota(jnp.int32, (2 * blk, width), 1) % HD
            key_doc = jnp.where(key < blk, docs_ref[2 * m], docs_ref[2 * m + 1])
            seen = (key - row <= block * blk - m * (2 * blk)) & (key_doc == docs_ref[block])
            bias[t] = jnp.where(seen, 0.0, masked_floor)

        def stored_at(b):
            place = jnp.int32(0)
            for r in range(blocks):
                place = place + r * (1 - jnp.minimum(jnp.abs(order_ref[r] - b), 1))
            return jnp.minimum(place, blocks - 1)

        def sort_blocks(kind, seq):
            for k in range(1, cycle):
                kv_copy(kind, k).wait_recv()
            for b in range(blocks):
                piece = gathered[kind][stored_at(b)]
                for g in range(kv_here):
                    part = piece[:, g * HD:(g + 1) * HD]
                    lanes = pl.ds((b % 2) * blk, blk)
                    seq[g, b // 2, lanes, :] = part
                    if kind == 0:
                        turned = part.astype(jnp.float32).T.astype(jnp.bfloat16)
                        kt_seq[g, b // 2, :, lanes] = turned

        def stacked(buf, c):
            halves = []
            for half in range(2):
                piece = buf[c, half * blk:(half + 1) * blk, :]
                halves.append(jnp.concatenate(
                    [piece[:, h * HD:(h + 1) * HD] for h in range(HEADS_AT_ONCE)], axis=0
                ))
            return choose(first_hi, *halves), choose(first_hi, *halves[::-1])

        def combine(values, op, empty):
            hi, lo = None, values[sure]
            for t in range(sure):
                hi = values[t] if hi is None else op(hi, values[t])
            for f in range(floats):
                value = values[sure + 1 + f]
                hi = op(hi, choose(float_hi[f], value, empty))
                lo = op(lo, choose(1 - float_hi[f], value, empty))
            return hi, lo

        sort_blocks(0, k_seq)

        @pl.loop(0, chunks)
        def _(c):
            q_copy(c).wait()
            g = c // per_kv
            hi_query, lo_query = stacked(q_buf, c)
            scores, tops = [], []
            for t in range(tasks):
                query = pick(t, hi_query, lo_query)
                s = dot(k_seq[g, super_of(t)], query, NT) * inverse + bias[t]
                scores.append(s)
                tops.append(jnp.max(s, axis=0, keepdims=True))
            hi_top, lo_top = combine(tops, jnp.maximum, masked_floor)
            weights = [jnp.exp(scores[t] - pick(t, hi_top, lo_top)) for t in range(tasks)]
            sums = [jnp.sum(w, axis=0, keepdims=True) for w in weights]
            hi_sum, lo_sum = combine(sums, jnp.add, 0.0)
            hi_over, lo_over = 1.0 / hi_sum, 1.0 / lo_sum
            for t in range(tasks):
                probs[c, t] = (weights[t] * pick(t, hi_over, lo_over)).astype(jnp.bfloat16)

        sort_blocks(1, v_seq)

        @pl.loop(0, chunks)
        def _(c):
            o_copy(c).wait()

        def block_copy(g, k):
            flat, device = peer(k)
            return pltpu.make_async_remote_copy(
                src_ref=send_buf.at[g, flat], dst_ref=recv_buf.at[g, me],
                send_sem=g_send.at[g, k], recv_sem=g_recv.at[g, k],
                device_id=device, device_id_type=MESH,
            )

        for g in range(kv_here):
            dk_acc[...] = jnp.zeros_like(dk_acc)
            dv_acc[...] = jnp.zeros_like(dv_acc)

            @pl.loop(g * per_kv, (g + 1) * per_kv)
            def _(c):
                z_copy(c).wait_recv()

                dots = []
                for half in range(2):
                    here_rows = slice(half * blk, (half + 1) * blk)
                    both = do_buf[c, here_rows, :].astype(jnp.float32) * o_buf[
                        c, here_rows, :
                    ].astype(jnp.float32)
                    dots.append(jnp.concatenate([
                        jnp.sum(both[:, h * HD:(h + 1) * HD].T, axis=0, keepdims=True)
                        for h in range(HEADS_AT_ONCE)
                    ], axis=1))
                hi_dots, lo_dots = choose(first_hi, *dots), choose(first_hi, *dots[::-1])
                hi_query, lo_query = stacked(q_buf, c)
                hi_grad, lo_grad = stacked(do_buf, c)
                turned = []
                for t in range(tasks):
                    m = super_of(t)
                    query = pick(t, hi_query, lo_query)
                    grad = pick(t, hi_grad, lo_grad)
                    low = probs[c, t]
                    dp = dot(v_seq[g, m], grad, NT) - pick(t, hi_dots, lo_dots)
                    ds = (low.astype(jnp.float32) * dp).astype(jnp.bfloat16)
                    slot = t if t < sure else (0 if t == sure else supers + t - sure - 1)
                    dv_acc[2 * slot:2 * slot + 2] += dot(low, grad).reshape(2, blk, HD)
                    dk_acc[2 * slot:2 * slot + 2] += dot(ds, query).reshape(2, blk, HD)
                    turned.append(dot(kt_seq[g, m], ds))
                hi_turned, lo_turned = combine(turned, jnp.add, 0.0)
                top = choose(first_hi, hi_turned, lo_turned) * inverse
                low_half = choose(first_hi, lo_turned, hi_turned) * inverse
                for h in range(HEADS_AT_ONCE):
                    cols = slice(h * HD, (h + 1) * HD)
                    dq_buf[c, 0:blk, cols] = top[:, cols].T.astype(jnp.bfloat16)
                    dq_buf[c, blk:2 * blk, cols] = low_half[:, cols].T.astype(jnp.bfloat16)
                dq_copy(c).start()

            for kind, acc in ((0, dk_acc), (1, dv_acc)):
                for f in range(floats):
                    extra = acc[2 * (supers + f):2 * (supers + f) + 2]
                    for m in range(supers):
                        hit = 1 - jnp.minimum(jnp.abs(float_super[f] - m), 1)
                        acc[2 * m:2 * m + 2] += choose(hit, extra, 0.0)
                for r in range(blocks):
                    piece = acc[order_ref[r]]
                    send_buf[g, r, kind * blk:(kind + 1) * blk, :] = piece.astype(jnp.bfloat16)
            recv_buf[g, me] = send_buf[g, me]
            for k in range(1, peers):
                block_copy(g, k).start()

        for g in range(kv_here):
            for k in range(1, peers):
                block_copy(g, k).wait_recv()
            for t in range(tps):
                total = recv_buf[g, t].astype(jnp.float32)
                for d in range(1, cycle):
                    total = total + recv_buf[g, d * tps + t].astype(jnp.float32)
                cols = slice((t * kv_here + g) * HD, (t * kv_here + g + 1) * HD)
                dk_out[0, :, cols] = (total[:blk] * inverse).astype(jnp.bfloat16)
                dv_out[0, :, cols] = total[blk:].astype(jnp.bfloat16)

        @pl.loop(0, chunks)
        def _(c):
            z_copy(c).wait_send()
            dq_copy(c).wait()

        for kind in range(2):
            for k in range(1, cycle):
                kv_copy(kind, k).wait_send()
        for g in range(kv_here):
            for k in range(1, peers):
                block_copy(g, k).wait_send()

    bf16, f32 = jnp.bfloat16, jnp.float32
    scratch = [
        pltpu.VMEM((chunks, rows, width), bf16),
        pltpu.VMEM((chunks, rows, width), bf16),
        pltpu.VMEM((chunks, rows, width), bf16),
        pltpu.VMEM((chunks, rows, width), bf16),
        pltpu.VMEM((blocks, blk, kv_here * HD), bf16),
        pltpu.VMEM((blocks, blk, kv_here * HD), bf16),
        pltpu.VMEM((kv_here, supers, 2 * blk, HD), bf16),
        pltpu.VMEM((kv_here, supers, 2 * blk, HD), bf16),
        pltpu.VMEM((kv_here, supers, HD, 2 * blk), bf16),
        pltpu.VMEM((tasks, 2 * blk, width), f32),
        pltpu.VMEM((chunks, tasks, 2 * blk, width), bf16),
        pltpu.VMEM((2 * (supers + floats), blk, HD), f32),
        pltpu.VMEM((2 * (supers + floats), blk, HD), f32),
        pltpu.VMEM((kv_here, peers, 2 * blk, HD), bf16),
        pltpu.VMEM((kv_here, peers, 2 * blk, HD), bf16),
        pltpu.SemaphoreType.DMA((chunks,)),
        pltpu.SemaphoreType.DMA((chunks,)),
        pltpu.SemaphoreType.DMA((chunks,)),
        pltpu.SemaphoreType.DMA((chunks,)),
        pltpu.SemaphoreType.DMA((chunks,)),
        pltpu.SemaphoreType.DMA((2, cycle)),
        pltpu.SemaphoreType.DMA((2, cycle)),
        pltpu.SemaphoreType.DMA((kv_here, peers)),
        pltpu.SemaphoreType.DMA((kv_here, peers)),
    ]
    pairs = heads * tasks * 2 * blk * blk
    smem = pl.BlockSpec(memory_space=pltpu.SMEM)
    vmem = pl.BlockSpec(memory_space=pltpu.VMEM)
    hbm = pl.BlockSpec(memory_space=pl.ANY)
    return pl.pallas_call(
        kernel,
        out_shape=(
            jax.ShapeDtypeStruct((1, rows, heads * HD), bf16),
            jax.ShapeDtypeStruct((1, rows // tps, KVH * HD), bf16),
            jax.ShapeDtypeStruct((1, rows // tps, KVH * HD), bf16),
        ),
        in_specs=[smem, smem, smem, vmem, vmem, hbm, hbm, hbm],
        out_specs=(hbm, vmem, vmem),
        scratch_shapes=scratch,
        compiler_params=pltpu.CompilerParams(
            collective_id=0, has_side_effects=True, vmem_limit_bytes=56 << 20
        ),
        cost_estimate=pl.CostEstimate(
            flops=5 * 2 * HD * pairs, bytes_accessed=5 * rows * heads * HD * 2,
            transcendentals=pairs,
        ),
    )


def solution(mesh):
    sizes = (mesh.shape["pipe"], mesh.shape["ctx"], mesh.shape["tp"])

    def on_device(
        queries, key_codes, value_codes, kv_scales, saved_out, section_grads, block_order, block_docs
    ):
        call = make_kernel(
            sizes, queries.shape[1], queries.shape[2] // HD, key_codes.shape[2] // HD,
            block_order.shape[0],
        )
        return call(
            block_order, block_docs, kv_scales, key_codes, value_codes, queries, saved_out,
            section_grads,
        )

    in_specs = (
        P("pipe", "ctx", "tp"),
        P("pipe", "ctx", "tp"),
        P("pipe", "ctx", "tp"),
        P("pipe", "ctx", None),
        P("pipe", "ctx", "tp"),
        P("pipe", "ctx", "tp"),
        P(),
        P(),
    )
    out_specs = (
        P("pipe", "ctx", "tp"),
        P("pipe", ("ctx", "tp"), None),
        P("pipe", ("ctx", "tp"), None),
    )
    return jax.shard_map(
        on_device, mesh=mesh, in_specs=in_specs, out_specs=out_specs, check_vma=False
    )
```

time: 169 us -> 68.1 us (0.40)
  matrix products: 85.2 us -> 0 us
  Pallas kernels: 0 us -> 62.8 us
  local copies, waits for them, and re-layouts: 33.4 us -> 4.49 us
  other arithmetic: 26.4 us -> 0 us
  starting transfers between devices: 11.5 us -> 0 us
  blocking collectives: 7.2 us -> 0 us
  waiting for transfers between devices: 2.86 us -> 0 us
    dot_general x21 -> x0, matrix products: 85.2 us -> none  [the longest x4 25.4 us: block_grads(): jnp.einsum('grij,jgd->igrd', dscores, key_piece, preferred_element_type=j...]
    pallas_call x0 -> x1, Pallas kernels: none -> 62.8 us  [on_device(): call(block_order, block_docs, kv_scales, key_codes, value_codes, queries,...]
    reduce_sum x12 -> x0, other arithmetic: 18.4 us -> none  [the longest x1 14.6 us: on_device(): new_sum = jnp.sum(weights, axis=-1)]
    while x11 -> x0, local copies, waits for them, and re-layouts: 14.2 us -> none
    unnamed x28 -> x7, local copies, waits for them, and re-layouts: 15.2 us -> 4.49 us
    ppermute x8 -> x0, starting transfers between devices: 8.09 us -> none  [from_behind(): lax.ppermute(array, axis, [(i, (i + by) % size) for i in range(size)])]
    all_gather x1 -> x0, blocking collectives: 7.2 us -> none  [on_device(): piece = lax.all_gather(keys, 'ctx', axis=0, tiled=True)]
    convert_element_type x4 -> x0, other arithmetic: 4.19 us -> none  [the longest x1 4.12 us: on_device(): grad_query.astype(jnp.bfloat16).reshape(1, rows_here, heads_here * HD)]
  transfers between devices with their start and end apart: 9 -> 0, of which waited for: 3 -> 0; matrix products, arithmetic and copies ran while one was open for 66% -> 0% of each run, Pallas kernels for 0% -> 0%
where the time goes in v1:
time: 68.1 us; the launch traced here: 67.9 us
  Pallas kernels  62.8 us (92%)
  local copies, waits for them, and re-layouts  4.49 us (7%)
    pallas_call x1, Pallas kernels, on_device(): call(block_order, block_docs, kv_scales, key_codes, value_codes, queries,...  62.8 us
    unnamed x7, local copies, waits for them, and re-layouts  4.49 us

profile of v1, /device:TPU:0, one launch (start us, length us, event | category | flops | bytes accessed | tf_op | source)
XLA Modules:
  0.0 67.9 jit_solution(12374566002589709132)
XLA Ops:
  0.6 62.8 %shard_map.103 = (bf16[1,256,4096]{2,1,0:T(8,128)(2,1)}, bf16[1,128,512]{2,1,0:T(8,128)(2,1)}, bf16[1,128,512]{2,1,0:T(8,128)(2,1)}) custom-call(s32[8]{0:T(128)} %order_ref.1, s32[8]{0:T(128)} %docs_ref.1, f32[1,2,8]{2,1,0:T(2,128)} %scales_ref.1, bf16[1,256,256]{2,1,0:T(8,128)(2,1)} %key_codes.1, bf16[1,256,256]{2,1,0:T(8,128)(2,1)} %value_codes.1, ...), custom_call_target="tpu_custom_call" | custom-call | flops 6710886400 | bytes 10485760 | tf_op jit(solution)/shard_map/pallas_call | solution.py:366
  63.4 0.0 copy-start.1
  63.4 0.0 copy-start
  63.4 3.2 %copy.14 = bf16[1,256,4096]{2,1,0:T(8,128)(2,1)} copy(bf16[1,256,4096]{2,1,0:T(8,128)(2,1)} %get-tuple-element.6) | data formatting | bytes 4194304
  66.6 0.0 copy-done.1
  66.6 0.7 copy.15
  67.3 0.0 copy-done
  67.3 0.7 copy.16
Async XLA Ops:
  63.4 3.2 %copy-start.1 = (bf16[1,128,512]{2,1,0:T(8,128)(2,1)S(1)}, bf16[1,128,512]{2,1,0:T(8,128)(2,1)}, u32[]{:S(2)}) copy-start(bf16[1,128,512]{2,1,0:T(8,128)(2,1)} %get-tuple-element.7) | copy-start | bytes 393220
  63.4 3.8 %copy-start = (bf16[1,128,512]{2,1,0:T(8,128)(2,1)S(1)}, bf16[1,128,512]{2,1,0:T(8,128)(2,1)}, u32[]{:S(2)}) copy-start(bf16[1,128,512]{2,1,0:T(8,128)(2,1)} %get-tuple-element.8) | copy-start | bytes 393220

commit v2 on v1

--- a/solution.py
+++ b/solution.py
@@ -9,6 +9,7 @@
 KVH = 4
 HD = 128
 HEADS_AT_ONCE = 2
+IN_FLIGHT = 4
 
 masked_floor = -1e30
 MESH = pl.DeviceIdType.MESH
@@ -26,6 +27,7 @@
     width = HEADS_AT_ONCE * HD
     chunks = heads // HEADS_AT_ONCE
     per_kv = chunks // kv_here
+    in_flight = min(chunks, IN_FLIGHT)
     supers = blocks // 2
     sure = blocks // 4 + 1
     floats = supers - sure
@@ -77,7 +79,7 @@
         def dq_copy(c):
             return pltpu.make_async_copy(dq_buf.at[c], columns(dq_out, c), dq_sem.at[c])
 
-        @pl.loop(0, chunks)
+        @pl.loop(0, in_flight)
         def _(c):
             z_copy(c).start()
 
@@ -231,6 +233,11 @@
             @pl.loop(g * per_kv, (g + 1) * per_kv)
             def _(c):
                 z_copy(c).wait_recv()
+                z_copy(c).wait_send()
+
+                @pl.when(c + in_flight < chunks)
+                def _():
+                    z_copy(c + in_flight).start()
 
                 dots = []
                 for half in range(2):
@@ -292,7 +299,6 @@
 
         @pl.loop(0, chunks)
         def _(c):
-            z_copy(c).wait_send()
             dq_copy(c).wait()
 
         for kind in range(2):

time: 68.1 us -> 72.8 us (1.069)
  Pallas kernels: 62.8 us -> 67.4 us
    pallas_call x1, Pallas kernels: 62.8 us -> 67.4 us  [on_device(): call(block_order, block_docs, kv_scales, key_codes, value_codes, queries,...]
where the time goes in v2:
time: 72.8 us; the launch traced here: 72.6 us
  Pallas kernels  67.4 us (93%)
  local copies, waits for them, and re-layouts  4.49 us (6%)
    pallas_call x1, Pallas kernels, on_device(): call(block_order, block_docs, kv_scales, key_codes, value_codes, queries,...  67.4 us
    unnamed x7, local copies, waits for them, and re-layouts  4.49 us

profile of v2, /device:TPU:0, one launch (start us, length us, event | category | flops | bytes accessed | tf_op | source)
XLA Modules:
  0.0 72.6 jit_solution(11870744641226251602)
XLA Ops:
  0.6 67.4 %shard_map.103 = (bf16[1,256,4096]{2,1,0:T(8,128)(2,1)}, bf16[1,128,512]{2,1,0:T(8,128)(2,1)}, bf16[1,128,512]{2,1,0:T(8,128)(2,1)}) custom-call(s32[8]{0:T(128)} %order_ref.1, s32[8]{0:T(128)} %docs_ref.1, f32[1,2,8]{2,1,0:T(2,128)} %scales_ref.1, bf16[1,256,256]{2,1,0:T(8,128)(2,1)} %key_codes.1, bf16[1,256,256]{2,1,0:T(8,128)(2,1)} %value_codes.1, ...), custom_call_target="tpu_custom_call" | custom-call | flops 6710886400 | bytes 10485760 | tf_op jit(solution)/shard_map/pallas_call | solution.py:372
  68.1 0.0 copy-start.1
  68.1 0.0 copy-start
  68.1 3.2 %copy.14 = bf16[1,256,4096]{2,1,0:T(8,128)(2,1)} copy(bf16[1,256,4096]{2,1,0:T(8,128)(2,1)} %get-tuple-element.6) | data formatting | bytes 4194304
  71.3 0.0 copy-done.1
  71.3 0.7 copy.15
  71.9 0.0 copy-done
  71.9 0.7 copy.16
Async XLA Ops:
  68.1 3.2 %copy-start.1 = (bf16[1,128,512]{2,1,0:T(8,128)(2,1)S(1)}, bf16[1,128,512]{2,1,0:T(8,128)(2,1)}, u32[]{:S(2)}) copy-start(bf16[1,128,512]{2,1,0:T(8,128)(2,1)} %get-tuple-element.7) | copy-start | bytes 393220
  68.1 3.8 %copy-start = (bf16[1,128,512]{2,1,0:T(8,128)(2,1)S(1)}, bf16[1,128,512]{2,1,0:T(8,128)(2,1)}, u32[]{:S(2)}) copy-start(bf16[1,128,512]{2,1,0:T(8,128)(2,1)} %get-tuple-element.8) | copy-start | bytes 393220

commit v3 on v2

--- a/solution.py
+++ b/solution.py
@@ -9,7 +9,8 @@
 KVH = 4
 HD = 128
 HEADS_AT_ONCE = 2
-IN_FLIGHT = 4
+IN_FLIGHT = 6
+LEAD = 2
 
 masked_floor = -1e30
 MESH = pl.DeviceIdType.MESH
@@ -27,7 +28,7 @@
     width = HEADS_AT_ONCE * HD
     chunks = heads // HEADS_AT_ONCE
     per_kv = chunks // kv_here
-    in_flight = min(chunks, IN_FLIGHT)
+    in_flight, lead = min(chunks, IN_FLIGHT), min(chunks, LEAD)
     supers = blocks // 2
     sure = blocks // 4 + 1
     floats = supers - sure
@@ -193,8 +194,7 @@
 
         sort_blocks(0, k_seq)
 
-        @pl.loop(0, chunks)
-        def _(c):
+        def find_probs(c):
             q_copy(c).wait()
             g = c // per_kv
             hi_query, lo_query = stacked(q_buf, c)
@@ -212,11 +212,11 @@
             for t in range(tasks):
                 probs[c, t] = (weights[t] * pick(t, hi_over, lo_over)).astype(jnp.bfloat16)
 
+        @pl.loop(0, lead)
+        def _(c):
+            find_probs(c)
+
         sort_blocks(1, v_seq)
-
-        @pl.loop(0, chunks)
-        def _(c):
-            o_copy(c).wait()
 
         def block_copy(g, k):
             flat, device = peer(k)
@@ -232,6 +232,11 @@
 
             @pl.loop(g * per_kv, (g + 1) * per_kv)
             def _(c):
+                @pl.when(c + lead < chunks)
+                def _():
+                    find_probs(c + lead)
+
+                o_copy(c).wait()
                 z_copy(c).wait_recv()
                 z_copy(c).wait_send()
 
@@ -359,6 +364,36 @@
     )
 
 
+def hand_over(*arrays):
+    pieces = 8
+
+    def kernel(*refs):
+        sources, targets, sems = refs[:len(arrays)], refs[len(arrays):-1], refs[-1]
+        copies = []
+        for source, target in zip(sources, targets):
+            count = pieces if source is sources[0] else 1
+            step = source.shape[1] // count
+            for i in range(count):
+                part = pl.ds(i * step, step)
+                copies.append(pltpu.make_async_copy(
+                    source.at[0, part], target.at[0, part], sems.at[len(copies)]
+                ))
+        for copy in copies:
+            copy.start()
+        for copy in copies:
+            copy.wait()
+
+    hbm = pl.BlockSpec(memory_space=pl.ANY)
+    return pl.pallas_call(
+        kernel,
+        out_shape=tuple(jax.ShapeDtypeStruct(a.shape, a.dtype) for a in arrays),
+        in_specs=[hbm] * len(arrays),
+        out_specs=(hbm,) * len(arrays),
+        scratch_shapes=[pltpu.SemaphoreType.DMA((pieces + len(arrays) - 1,))],
+        compiler_params=pltpu.CompilerParams(vmem_limit_bytes=56 << 20),
+    )(*arrays)
+
+
 def solution(mesh):
     sizes = (mesh.shape["pipe"], mesh.shape["ctx"], mesh.shape["tp"])
 
@@ -369,10 +404,10 @@
             sizes, queries.shape[1], queries.shape[2] // HD, key_codes.shape[2] // HD,
             block_order.shape[0],
         )
-        return call(
+        return hand_over(*call(
             block_order, block_docs, kv_scales, key_codes, value_codes, queries, saved_out,
             section_grads,
-        )
+        ))
 
     in_specs = (
         P("pipe", "ctx", "tp"),

time: 72.8 us -> 136 us (1.87)
  Pallas kernels: 67.4 us -> 135 us
  local copies, waits for them, and re-layouts: 4.49 us -> 0 us
    pallas_call x0 -> x1, Pallas kernels: none -> 72.7 us  [hand_over(): pl.pallas_call(kernel, out_shape=tuple((jax.ShapeDtypeStruct(a.shape, a.d...]
    pallas_call x1, Pallas kernels: 67.4 us -> 62.8 us  [on_device(): call(block_order, block_docs, kv_scales, key_codes, value_codes, queries,...]
    unnamed x7 -> x0, local copies, waits for them, and re-layouts: 4.49 us -> none
where the time goes in v3:
time: 136 us
  Pallas kernels  135 us (99%)
    pallas_call x1, Pallas kernels, hand_over(): pl.pallas_call(kernel, out_shape=tuple((jax.ShapeDtypeStruct(a.shape, a.d...  72.7 us
    pallas_call x1, Pallas kernels, on_device(): call(block_order, block_docs, kv_scales, key_codes, value_codes, queries,...  62.8 us

profile of v3, /device:TPU:0, one launch (start us, length us, event | category | flops | bytes accessed | tf_op | source)
XLA Modules:
  0.0 136.1 jit_solution(18086169584468393350)
XLA Ops:
  0.6 62.8 %shard_map.103 = (bf16[1,256,4096]{2,1,0:T(8,128)(2,1)}, bf16[1,128,512]{2,1,0:T(8,128)(2,1)}, bf16[1,128,512]{2,1,0:T(8,128)(2,1)}) custom-call(s32[8]{0:T(128)} %order_ref.1, s32[8]{0:T(128)} %docs_ref.1, f32[1,2,8]{2,1,0:T(2,128)} %scales_ref.1, bf16[1,256,256]{2,1,0:T(8,128)(2,1)} %key_codes.1, bf16[1,256,256]{2,1,0:T(8,128)(2,1)} %value_codes.1, ...), custom_call_target="tpu_custom_call" | custom-call | flops 6710886400 | bytes 10485760 | tf_op jit(solution)/shard_map/pallas_call | solution.py:407
  63.4 72.7 %shard_map.104 = (bf16[1,256,4096]{2,1,0:T(8,128)(2,1)}, bf16[1,128,512]{2,1,0:T(8,128)(2,1)}, bf16[1,128,512]{2,1,0:T(8,128)(2,1)}) custom-call(bf16[1,256,4096]{2,1,0:T(8,128)(2,1)} %get-tuple-element.6.refs_0_, bf16[1,128,512]{2,1,0:T(8,128)(2,1)} %get-tuple-element.7.refs_1_, bf16[1,128,512]{2,1,0:T(8,128)(2,1)} %get-tuple-element.8.refs_2_), custom_call_target="tpu_custom_call" | custom-call | tf_op jit(solution)/shard_map/pallas_call | solution.py:387

commit v4 on v3

--- a/solution.py
+++ b/solution.py
@@ -9,12 +9,12 @@
 KVH = 4
 HD = 128
 HEADS_AT_ONCE = 2
-IN_FLIGHT = 6
-LEAD = 2
+LEAD = 1
 
 masked_floor = -1e30
 MESH = pl.DeviceIdType.MESH
 NT = (((1,), (1,)), ((), ()))
+LOG2_E = 1.4426950408889634
 NN = (((1,), (0,)), ((), ()))
 
 
@@ -28,7 +28,7 @@
     width = HEADS_AT_ONCE * HD
     chunks = heads // HEADS_AT_ONCE
     per_kv = chunks // kv_here
-    in_flight, lead = min(chunks, IN_FLIGHT), min(chunks, LEAD)
+    lead = LEAD
     supers = blocks // 2
     sure = blocks // 4 + 1
     floats = supers - sure
@@ -80,7 +80,7 @@
         def dq_copy(c):
             return pltpu.make_async_copy(dq_buf.at[c], columns(dq_out, c), dq_sem.at[c])
 
-        @pl.loop(0, in_flight)
+        @pl.loop(0, chunks)
         def _(c):
             z_copy(c).start()
 
@@ -135,24 +135,34 @@
                 return t
             return 0 if t == sure else float_super[t - sure - 1]
 
-        def pick(t, hi, lo):
-            if t < sure:
-                return hi
-            if t == sure:
-                return lo
-            flag = float_hi[t - sure - 1]
+        groups = [(0, sure), (sure, sure + 1)] + [(t, t + 1) for t in range(sure + 1, tasks)]
+
+        def of_group(ref, g, u):
+            if u == 0:
+                return ref[g, 0:sure].reshape(sure * 2 * blk, HD)
+            return ref[g, super_of(groups[u][0])]
+
+        def turned_of_group(g, u):
+            if u == 0:
+                return jnp.concatenate([kt_seq[g, m] for m in range(sure)], axis=1)
+            return kt_seq[g, super_of(groups[u][0])]
+
+        def pick(u, hi, lo):
+            if u < 2:
+                return lo if u else hi
+            flag = float_hi[u - 2]
             if hi.shape == ():
                 return flag * hi + (1 - flag) * lo
             return choose(flag, hi, lo)
 
         for t in range(tasks):
             m = super_of(t)
-            block = pick(t, hi_block, lo_block)
+            block = pick(max(t - sure + 1, 0), hi_block, lo_block)
             key = lax.broadcasted_iota(jnp.int32, (2 * blk, width), 0)
             row = lax.broadcasted_iota(jnp.int32, (2 * blk, width), 1) % HD
             key_doc = jnp.where(key < blk, docs_ref[2 * m], docs_ref[2 * m + 1])
             seen = (key - row <= block * blk - m * (2 * blk)) & (key_doc == docs_ref[block])
-            bias[t] = jnp.where(seen, 0.0, masked_floor)
+            bias[t * 2 * blk:(t + 1) * 2 * blk] = jnp.where(seen, 0.0, masked_floor)
 
         def stored_at(b):
             place = jnp.int32(0)
@@ -183,11 +193,9 @@
             return choose(first_hi, *halves), choose(first_hi, *halves[::-1])
 
         def combine(values, op, empty):
-            hi, lo = None, values[sure]
-            for t in range(sure):
-                hi = values[t] if hi is None else op(hi, values[t])
+            hi, lo = values[0], values[1]
             for f in range(floats):
-                value = values[sure + 1 + f]
+                value = values[2 + f]
                 hi = op(hi, choose(float_hi[f], value, empty))
                 lo = op(lo, choose(1 - float_hi[f], value, empty))
             return hi, lo
@@ -195,25 +203,27 @@
         sort_blocks(0, k_seq)
 
         def find_probs(c):
-            q_copy(c).wait()
             g = c // per_kv
             hi_query, lo_query = stacked(q_buf, c)
             scores, tops = [], []
-            for t in range(tasks):
-                query = pick(t, hi_query, lo_query)
-                s = dot(k_seq[g, super_of(t)], query, NT) * inverse + bias[t]
+            for u, (begin, end) in enumerate(groups):
+                query = pick(u, hi_query, lo_query)
+                part = slice(begin * 2 * blk, end * 2 * blk)
+                s = dot(of_group(k_seq, g, u), query, NT) * (inverse * LOG2_E) + bias[part]
                 scores.append(s)
                 tops.append(jnp.max(s, axis=0, keepdims=True))
             hi_top, lo_top = combine(tops, jnp.maximum, masked_floor)
-            weights = [jnp.exp(scores[t] - pick(t, hi_top, lo_top)) for t in range(tasks)]
+            weights = [jnp.exp2(s - pick(u, hi_top, lo_top)) for u, s in enumerate(scores)]
             sums = [jnp.sum(w, axis=0, keepdims=True) for w in weights]
             hi_sum, lo_sum = combine(sums, jnp.add, 0.0)
             hi_over, lo_over = 1.0 / hi_sum, 1.0 / lo_sum
-            for t in range(tasks):
-                probs[c, t] = (weights[t] * pick(t, hi_over, lo_over)).astype(jnp.bfloat16)
+            for u, (begin, end) in enumerate(groups):
+                part = slice(begin * 2 * blk, end * 2 * blk)
+                probs[c, part] = (weights[u] * pick(u, hi_over, lo_over)).astype(jnp.bfloat16)
 
         @pl.loop(0, lead)
         def _(c):
+            q_copy(c).wait()
             find_probs(c)
 
         sort_blocks(1, v_seq)
@@ -230,20 +240,12 @@
             dk_acc[...] = jnp.zeros_like(dk_acc)
             dv_acc[...] = jnp.zeros_like(dv_acc)
 
-            @pl.loop(g * per_kv, (g + 1) * per_kv)
-            def _(c):
-                @pl.when(c + lead < chunks)
-                def _():
-                    find_probs(c + lead)
-
+            def backward(c, more):
                 o_copy(c).wait()
                 z_copy(c).wait_recv()
-                z_copy(c).wait_send()
-
-                @pl.when(c + in_flight < chunks)
-                def _():
-                    z_copy(c + in_flight).start()
-
+                if more:
+                    q_copy(c + lead).wait()
+                    find_probs(c + lead)
                 dots = []
                 for half in range(2):
                     here_rows = slice(half * blk, (half + 1) * blk)
@@ -258,17 +260,17 @@
                 hi_query, lo_query = stacked(q_buf, c)
                 hi_grad, lo_grad = stacked(do_buf, c)
                 turned = []
-                for t in range(tasks):
-                    m = super_of(t)
-                    query = pick(t, hi_query, lo_query)
-                    grad = pick(t, hi_grad, lo_grad)
-                    low = probs[c, t]
-                    dp = dot(v_seq[g, m], grad, NT) - pick(t, hi_dots, lo_dots)
+                for u, (begin, end) in enumerate(groups):
+                    query = pick(u, hi_query, lo_query)
+                    grad = pick(u, hi_grad, lo_grad)
+                    low = probs[c, begin * 2 * blk:end * 2 * blk]
+                    dp = dot(of_group(v_seq, g, u), grad, NT) - pick(u, hi_dots, lo_dots)
                     ds = (low.astype(jnp.float32) * dp).astype(jnp.bfloat16)
-                    slot = t if t < sure else (0 if t == sure else supers + t - sure - 1)
-                    dv_acc[2 * slot:2 * slot + 2] += dot(low, grad).reshape(2, blk, HD)
-                    dk_acc[2 * slot:2 * slot + 2] += dot(ds, query).reshape(2, blk, HD)
-                    turned.append(dot(kt_seq[g, m], ds))
+                    first_slot = 0 if u < 2 else supers + u - 2
+                    slots = slice(2 * first_slot, 2 * (first_slot + end - begin))
+                    dv_acc[slots] += dot(low, grad).reshape(2 * (end - begin), blk, HD)
+                    dk_acc[slots] += dot(ds, query).reshape(2 * (end - begin), blk, HD)
+                    turned.append(dot(turned_of_group(g, u), ds))
                 hi_turned, lo_turned = combine(turned, jnp.add, 0.0)
                 top = choose(first_hi, hi_turned, lo_turned) * inverse
                 low_half = choose(first_hi, lo_turned, hi_turned) * inverse
@@ -277,6 +279,17 @@
                     dq_buf[c, 0:blk, cols] = top[:, cols].T.astype(jnp.bfloat16)
                     dq_buf[c, blk:2 * blk, cols] = low_half[:, cols].T.astype(jnp.bfloat16)
                 dq_copy(c).start()
+
+            stop = min((g + 1) * per_kv, chunks - lead)
+
+            @pl.loop(g * per_kv, stop)
+            def _(c):
+                backward(c, True)
+
+            if stop < (g + 1) * per_kv:
+                @pl.loop(stop, (g + 1) * per_kv)
+                def _(c):
+                    backward(c, False)
 
             for kind, acc in ((0, dk_acc), (1, dv_acc)):
                 for f in range(floats):
@@ -304,6 +317,7 @@
 
         @pl.loop(0, chunks)
         def _(c):
+            z_copy(c).wait_send()
             dq_copy(c).wait()
 
         for kind in range(2):
@@ -324,8 +338,8 @@
         pltpu.VMEM((kv_here, supers, 2 * blk, HD), bf16),
         pltpu.VMEM((kv_here, supers, 2 * blk, HD), bf16),
         pltpu.VMEM((kv_here, supers, HD, 2 * blk), bf16),
-        pltpu.VMEM((tasks, 2 * blk, width), f32),
-        pltpu.VMEM((chunks, tasks, 2 * blk, width), bf16),
+        pltpu.VMEM((tasks * 2 * blk, width), f32),
+        pltpu.VMEM((chunks, tasks * 2 * blk, width), bf16),
         pltpu.VMEM((2 * (supers + floats), blk, HD), f32),
         pltpu.VMEM((2 * (supers + floats), blk, HD), f32),
         pltpu.VMEM((kv_here, peers, 2 * blk, HD), bf16),
@@ -367,20 +381,29 @@
 def hand_over(*arrays):
     pieces = 8
 
+    count = len(arrays)
+
     def kernel(*refs):
-        sources, targets, sems = refs[:len(arrays)], refs[len(arrays):-1], refs[-1]
-        copies = []
-        for source, target in zip(sources, targets):
-            count = pieces if source is sources[0] else 1
-            step = source.shape[1] // count
-            for i in range(count):
-                part = pl.ds(i * step, step)
-                copies.append(pltpu.make_async_copy(
-                    source.at[0, part], target.at[0, part], sems.at[len(copies)]
+        sources, targets, held = refs[:count], refs[count:2 * count], refs[2 * count:3 * count]
+        in_sems, out_sems = refs[3 * count:]
+        inward, outward = [], []
+        for source, target, middle in zip(sources, targets, held):
+            parts = pieces if source is sources[0] else 1
+            step = source.shape[1] // parts
+            for i in range(parts):
+                part, at = pl.ds(i * step, step), len(inward)
+                inward.append(pltpu.make_async_copy(
+                    source.at[0, part], middle.at[part], in_sems.at[at]
                 ))
-        for copy in copies:
+                outward.append(pltpu.make_async_copy(
+                    middle.at[part], target.at[0, part], out_sems.at[at]
+                ))
+        for copy in inward:
             copy.start()
-        for copy in copies:
+        for copy, onward in zip(inward, outward):
+            copy.wait()
+            onward.start()
+        for copy in outward:
             copy.wait()
 
     hbm = pl.BlockSpec(memory_space=pl.ANY)
@@ -389,7 +412,8 @@
         out_shape=tuple(jax.ShapeDtypeStruct(a.shape, a.dtype) for a in arrays),
         in_specs=[hbm] * len(arrays),
         out_specs=(hbm,) * len(arrays),
-        scratch_shapes=[pltpu.SemaphoreType.DMA((pieces + len(arrays) - 1,))],
+        scratch_shapes=[pltpu.VMEM(a.shape[1:], a.dtype) for a in arrays]
+        + [pltpu.SemaphoreType.DMA((pieces + count - 1,))] * 2,
         compiler_params=pltpu.CompilerParams(vmem_limit_bytes=56 << 20),
     )(*arrays)
 

time: 136 us -> 65.9 us (0.48)
  Pallas kernels: 135 us -> 65.1 us
    pallas_call x1, Pallas kernels: 72.7 us -> 2.51 us  [hand_over(): pl.pallas_call(kernel, out_shape=tuple((jax.ShapeDtypeStruct(a.shape, a.d...]
where the time goes in v4:
time: 65.9 us; the launch traced here: 65.7 us
  Pallas kernels  65.1 us (99%)
    pallas_call x1, Pallas kernels, on_device(): call(block_order, block_docs, kv_scales, key_codes, value_codes, queries,...  62.6 us
    pallas_call x1, Pallas kernels, hand_over(): pl.pallas_call(kernel, out_shape=tuple((jax.ShapeDtypeStruct(a.shape, a.d...  2.51 us

profile of v4, /device:TPU:0, one launch (start us, length us, event | category | flops | bytes accessed | tf_op | source)
XLA Modules:
  0.0 65.7 jit_solution(11251187440365451382)
XLA Ops:
  0.6 62.6 %shard_map.103 = (bf16[1,256,4096]{2,1,0:T(8,128)(2,1)}, bf16[1,128,512]{2,1,0:T(8,128)(2,1)}, bf16[1,128,512]{2,1,0:T(8,128)(2,1)}) custom-call(s32[8]{0:T(128)} %order_ref.1, s32[8]{0:T(128)} %docs_ref.1, f32[1,2,8]{2,1,0:T(2,128)} %scales_ref.1, bf16[1,256,256]{2,1,0:T(8,128)(2,1)} %key_codes.1, bf16[1,256,256]{2,1,0:T(8,128)(2,1)} %value_codes.1, ...), custom_call_target="tpu_custom_call" | custom-call | flops 6710886400 | bytes 10485760 | tf_op jit(solution)/shard_map/pallas_call | solution.py:431
  63.2 2.5 %shard_map.104 = (bf16[1,256,4096]{2,1,0:T(8,128)(2,1)}, bf16[1,128,512]{2,1,0:T(8,128)(2,1)}, bf16[1,128,512]{2,1,0:T(8,128)(2,1)}) custom-call(bf16[1,256,4096]{2,1,0:T(8,128)(2,1)} %get-tuple-element.6.refs_0_, bf16[1,128,512]{2,1,0:T(8,128)(2,1)} %get-tuple-element.7.refs_1_, bf16[1,128,512]{2,1,0:T(8,128)(2,1)} %get-tuple-element.8.refs_2_), custom_call_target="tpu_custom_call" | custom-call | tf_op jit(solution)/shard_map/pallas_call | solution.py:410

commit v5 on v4

--- a/solution.py
+++ b/solution.py
@@ -259,7 +259,7 @@
                 hi_dots, lo_dots = choose(first_hi, *dots), choose(first_hi, *dots[::-1])
                 hi_query, lo_query = stacked(q_buf, c)
                 hi_grad, lo_grad = stacked(do_buf, c)
-                turned = []
+                changes = []
                 for u, (begin, end) in enumerate(groups):
                     query = pick(u, hi_query, lo_query)
                     grad = pick(u, hi_grad, lo_grad)
@@ -270,7 +270,13 @@
                     slots = slice(2 * first_slot, 2 * (first_slot + end - begin))
                     dv_acc[slots] += dot(low, grad).reshape(2 * (end - begin), blk, HD)
                     dk_acc[slots] += dot(ds, query).reshape(2 * (end - begin), blk, HD)
-                    turned.append(dot(turned_of_group(g, u), ds))
+                    changes.append(ds)
+                if more:
+                    finish(c, changes)
+                return changes
+
+            def finish(c, changes):
+                turned = [dot(turned_of_group(g, u), ds) for u, ds in enumerate(changes)]
                 hi_turned, lo_turned = combine(turned, jnp.add, 0.0)
                 top = choose(first_hi, hi_turned, lo_turned) * inverse
                 low_half = choose(first_hi, lo_turned, hi_turned) * inverse
@@ -286,10 +292,9 @@
             def _(c):
                 backward(c, True)
 
-            if stop < (g + 1) * per_kv:
-                @pl.loop(stop, (g + 1) * per_kv)
-                def _(c):
-                    backward(c, False)
+            last = chunks - 1 if stop < (g + 1) * per_kv else None
+            if last is not None:
+                changes = backward(last, False)
 
             for kind, acc in ((0, dk_acc), (1, dv_acc)):
                 for f in range(floats):
@@ -297,12 +302,19 @@
                     for m in range(supers):
                         hit = 1 - jnp.minimum(jnp.abs(float_super[f] - m), 1)
                         acc[2 * m:2 * m + 2] += choose(hit, extra, 0.0)
-                for r in range(blocks):
-                    piece = acc[order_ref[r]]
-                    send_buf[g, r, kind * blk:(kind + 1) * blk, :] = piece.astype(jnp.bfloat16)
+
+            def prepare(r):
+                b = order_ref[r]
+                send_buf[g, r, 0:blk, :] = dk_acc[b].astype(jnp.bfloat16)
+                send_buf[g, r, blk:2 * blk, :] = dv_acc[b].astype(jnp.bfloat16)
+
+            for k in range(1, peers):
+                prepare(peer(k)[0])
+                block_copy(g, k).start()
+            prepare(me)
             recv_buf[g, me] = send_buf[g, me]
-            for k in range(1, peers):
-                block_copy(g, k).start()
+            if last is not None:
+                finish(last, changes)
 
         for g in range(kv_here):
             for k in range(1, peers):

time: 65.9 us -> 65.7 us (level)
  no operation moved by 1% of the time
where the time goes in v5:
time: 65.7 us; the launch traced here: 65.5 us
  Pallas kernels  64.9 us (99%)
    pallas_call x1, Pallas kernels, on_device(): call(block_order, block_docs, kv_scales, key_codes, value_codes, queries,...  62.4 us
    pallas_call x1, Pallas kernels, hand_over(): pl.pallas_call(kernel, out_shape=tuple((jax.ShapeDtypeStruct(a.shape, a.d...  2.51 us

profile of v5, /device:TPU:0, one launch (start us, length us, event | category | flops | bytes accessed | tf_op | source)
XLA Modules:
  0.0 65.5 jit_solution(14700739282536055688)
XLA Ops:
  0.6 62.4 %shard_map.103 = (bf16[1,256,4096]{2,1,0:T(8,128)(2,1)}, bf16[1,128,512]{2,1,0:T(8,128)(2,1)}, bf16[1,128,512]{2,1,0:T(8,128)(2,1)}) custom-call(s32[8]{0:T(128)} %order_ref.1, s32[8]{0:T(128)} %docs_ref.1, f32[1,2,8]{2,1,0:T(2,128)} %scales_ref.1, bf16[1,256,256]{2,1,0:T(8,128)(2,1)} %key_codes.1, bf16[1,256,256]{2,1,0:T(8,128)(2,1)} %value_codes.1, ...), custom_call_target="tpu_custom_call" | custom-call | flops 6710886400 | bytes 10485760 | tf_op jit(solution)/shard_map/pallas_call | solution.py:443
  63.0 2.5 %shard_map.104 = (bf16[1,256,4096]{2,1,0:T(8,128)(2,1)}, bf16[1,128,512]{2,1,0:T(8,128)(2,1)}, bf16[1,128,512]{2,1,0:T(8,128)(2,1)}) custom-call(bf16[1,256,4096]{2,1,0:T(8,128)(2,1)} %get-tuple-element.6.refs_0_, bf16[1,128,512]{2,1,0:T(8,128)(2,1)} %get-tuple-element.7.refs_1_, bf16[1,128,512]{2,1,0:T(8,128)(2,1)} %get-tuple-element.8.refs_2_), custom_call_target="tpu_custom_call" | custom-call | tf_op jit(solution)/shard_map/pallas_call | solution.py:422
